TPU v7x, 32 devices: a whole 2x2x4 slice. The times are simulated.
32 devices in a mesh: row: 8 (over y, x, core), col: 4 (over z).
Axes of the slice: x: 2, y: 2, z: 4, core: 2. Of those that a mesh axis runs over, the one named last changes fastest.
Arguments:
- features: bfloat16 [32, 1024, 1024], P(None, 'row', 'col'), may hold values from -45 to 45
- first_kernel: bfloat16 [3, 3, 32, 32], replicated, may hold values from -0.375 to 0.375
- second_kernel: bfloat16 [3, 3, 32, 32], replicated, may hold values from -0.375 to 0.375
- first_gain: float32 [32], replicated, may hold values from 0.5 to 1.5
- first_shift: float32 [32], replicated, may hold values from -3 to 3
- second_gain: float32 [32], replicated, may hold values from 0.5 to 1.5
- second_shift: float32 [32], replicated, may hold values from -3 to 3
Outputs:
- symmetric_map: bfloat16 [32, 1024, 1024], P(None, 'row', 'col')
All inputs are finite; a program needn't handle non-finite values.
Results may differ from a plain program's by a relative error of at most 0.0053.
Values may be sent and summed in bfloat16 or wider, within the bound.
A program may use at most 192 MiB of HBM per device.

v0:
```python
import functools

import jax
import jax.numpy as jnp
from jax import lax
from jax.experimental import pallas as pl
from jax.experimental.pallas import tpu as pltpu
from jax.sharding import PartitionSpec as P

STEP = 8
GROUP = 4
EPSILON = 1e-05
LANES = 128
MESH = pl.DeviceIdType.MESH


def iota(dim):
    return lax.broadcasted_iota(jnp.int32, (LANES, LANES), dim)


def one_hot(mask):
    return jnp.where(mask, 1.0, 0.0).astype(jnp.bfloat16)


def dot(a, b):
    return jnp.dot(a, b, preferred_element_type=jnp.float32)


def block_kernel(
    rows,
    cols,
    x_ref,
    first_ref,
    second_ref,
    scales_ref,
    out_ref,
    pad_one,
    pad_two,
    hidden,
    packed,
    strips,
    col_stats,
    row_stats,
    row_send,
    row_recv,
    col_send,
    col_recv,
    cs_send,
    cs_recv,
    rs_send,
    rs_recv,
):
    row = lax.axis_index("row")
    col = lax.axis_index("col")
    phases, depth, width = x_ref.shape
    chans = scales_ref.shape[1]
    count = depth // chans
    full = depth + 2 * chans
    cells = float(phases * count * width)
    centre = pl.ds(LANES, width)

    barrier = pltpu.get_barrier_semaphore()
    for d in range(1, cols):
        pl.semaphore_signal(
            barrier, inc=1, device_id=(row, lax.rem(col + d, cols)), device_id_type=MESH
        )
    for d in range(1, rows):
        pl.semaphore_signal(
            barrier, inc=1, device_id=(lax.rem(row + d, rows), col), device_id_type=MESH
        )
    pl.semaphore_wait(barrier, rows + cols - 2)

    def row_copy(pad, n, down):
        source = depth if down else chans
        target = 0 if down else depth + chans
        device = jnp.minimum(row + 1, rows - 1) if down else jnp.maximum(row - 1, 0)
        slot = 2 * n + int(down)
        return pltpu.make_async_remote_copy(
            src_ref=pad.at[:, pl.ds(source, chans), centre],
            dst_ref=pad.at[:, pl.ds(target, chans), centre],
            send_sem=row_send.at[slot],
            recv_sem=row_recv.at[slot],
            device_id=(device, col),
            device_id_type=MESH,
        )

    def col_copy(n, right):
        device = jnp.minimum(col + 1, cols - 1) if right else jnp.maximum(col - 1, 0)
        slot = 2 * n + int(right)
        return pltpu.make_async_remote_copy(
            src_ref=packed.at[n],
            dst_ref=strips.at[slot],
            send_sem=col_send.at[slot],
            recv_sem=col_recv.at[slot],
            device_id=(row, device),
            device_id_type=MESH,
        )

    def halo(pad, n):
        up, down = row_copy(pad, n, False), row_copy(pad, n, True)
        left, right = col_copy(n, False), col_copy(n, True)
        has_up, has_down = row > 0, row < rows - 1
        has_left, has_right = col > 0, col < cols - 1

        @pl.when(has_up)
        def _():
            up.start()

        @pl.when(has_down)
        def _():
            down.start()

        blank = jnp.zeros((phases, chans, width), jnp.bfloat16)

        @pl.when(jnp.logical_not(has_up))
        def _():
            pad[:, pl.ds(0, chans), centre] = blank

        @pl.when(jnp.logical_not(has_down))
        def _():
            pad[:, pl.ds(depth + chans, chans), centre] = blank

        @pl.when(jnp.logical_not(has_left))
        def _():
            strips[2 * n + 1] = jnp.zeros((full, LANES), jnp.bfloat16)

        @pl.when(jnp.logical_not(has_right))
        def _():
            strips[2 * n] = jnp.zeros((full, LANES), jnp.bfloat16)

        @pl.when(has_up)
        def _():
            down.wait_recv()
            up.wait_send()

        @pl.when(has_down)
        def _():
            up.wait_recv()
            down.wait_send()

        total = jnp.zeros((full, LANES), jnp.float32)
        i, j = iota(0), iota(1)
        edge = LANES - STEP
        for phase in range(phases):
            at = phase * STEP
            tail = one_hot((i >= edge) & (j == i - edge + at))
            head = one_hot((i < STEP) & (j == i + LANES // 2 + at))
            total += dot(pad[phase, :, pl.ds(width, LANES)], tail)
            total += dot(pad[phase, :, pl.ds(LANES, LANES)], head)
        packed[n] = total.astype(jnp.bfloat16)

        @pl.when(has_left)
        def _():
            left.start()

        @pl.when(has_right)
        def _():
            right.start()

        @pl.when(has_left)
        def _():
            right.wait_recv()
            left.wait_send()

        @pl.when(has_right)
        def _():
            left.wait_recv()
            right.wait_send()

        for phase in range(phases):
            at = phase * STEP
            tail = one_hot((j >= edge) & (i == j - edge + at))
            head = one_hot((j < STEP) & (i == j + LANES // 2 + at))
            pad[phase, :, pl.ds(0, LANES)] = dot(strips[2 * n + 1], tail).astype(jnp.bfloat16)
            pad[phase, :, pl.ds(width + LANES, LANES)] = dot(strips[2 * n], head).astype(
                jnp.bfloat16
            )

    def fold(values):
        total = jnp.sum(values.reshape(-1, chans, width), axis=0)
        return sum(total[:, k : k + LANES] for k in range(0, width, LANES))

    def conv(pad, weights):
        def body(phase, acc):
            shifted = [
                pad[phase, :, pl.ds(LANES + (b - 1) * STEP, width)] for b in range(3)
            ]
            for g in range(count // GROUP):
                low = g * GROUP * chans
                high = low + (GROUP + 2) * chans
                stacked = jnp.concatenate([s[low:high] for s in shifted], axis=0)
                part = dot(weights[...], stacked)
                hidden[phase, pl.ds(low, GROUP * chans), :] = part
                acc = acc + fold(part)
            return acc

        return lax.fori_loop(0, phases, body, jnp.zeros((chans, LANES), jnp.float32))

    def merge(own, other, size, stats, send, recv, n, axis_size, along_row):
        base = n * axis_size
        stats[base, pl.ds(0, chans), :] = own
        stats[base, pl.ds(chans, chans), :] = other
        copies = []
        for d in range(1, axis_size):
            device = (
                (lax.rem(row + d, axis_size), col)
                if along_row
                else (row, lax.rem(col + d, axis_size))
            )
            copy = pltpu.make_async_remote_copy(
                src_ref=stats.at[base],
                dst_ref=stats.at[base + d],
                send_sem=send.at[base + d],
                recv_sem=recv.at[base + d],
                device_id=device,
                device_id_type=MESH,
            )
            copy.start()
            copies.append(copy)
        for copy in copies:
            copy.wait()
        means = [stats[base + d, pl.ds(0, chans), :] for d in range(axis_size)]
        mean = sum(means) / axis_size
        squares = sum(stats[base + d, pl.ds(chans, chans), :] for d in range(axis_size))
        spread = sum((m - mean) * (m - mean) for m in means)
        return mean, squares + size * spread

    def norm(acc, n):
        own = jnp.broadcast_to(jnp.sum(acc, axis=1, keepdims=True) / cells, (chans, LANES))
        wide = jnp.concatenate([own] * (width // LANES), axis=1)

        def body(phase, squares):
            for q in range(count):
                diff = hidden[phase, pl.ds(q * chans, chans), :] - wide
                squares = squares + fold(diff * diff)
            return squares

        squares = lax.fori_loop(0, phases, body, jnp.zeros((chans, LANES), jnp.float32))
        squares = jnp.broadcast_to(jnp.sum(squares, axis=1, keepdims=True), (chans, LANES))
        mean, squares = merge(
            own, squares, cells, col_stats, cs_send, cs_recv, n, cols, False
        )
        mean, squares = merge(
            mean, squares, cells * cols, row_stats, rs_send, rs_recv, n, rows, True
        )
        factor = scales_ref[2 * n] * lax.rsqrt(squares / (cells * (rows * cols)) + EPSILON)
        shift = scales_ref[2 * n + 1]
        repeat = lambda v: jnp.concatenate([v] * (width // LANES), axis=1)
        return repeat(mean), repeat(factor), repeat(shift)

    pad_one[:, pl.ds(chans, depth), centre] = x_ref[...]
    halo(pad_one, 0)
    mean, factor, shift = norm(conv(pad_one, first_ref), 0)

    def activate(phase, carry):
        for q in range(count):
            cell = hidden[phase, pl.ds(q * chans, chans), :]
            cell = jnp.maximum((cell - mean) * factor + shift, 0.0)
            pad_two[phase, pl.ds((q + 1) * chans, chans), centre] = cell.astype(jnp.bfloat16)
        return carry

    lax.fori_loop(0, phases, activate, 0)
    halo(pad_two, 1)
    mean, factor, shift = norm(conv(pad_two, second_ref), 1)

    def finish(phase, carry):
        for q in range(count):
            at = pl.ds(q * chans, chans)
            cell = (hidden[phase, at, :] - mean) * factor + shift
            out_ref[phase, at, :] = (x_ref[phase, at, :].astype(jnp.float32) + cell).astype(
                jnp.bfloat16
            )
        return carry

    lax.fori_loop(0, phases, finish, 0)


def banded(kernel):
    taps = jnp.transpose(kernel, (2, 1, 0, 3))
    rows = [
        jnp.pad(taps, ((0, 0), (0, 0), (q, GROUP - 1 - q), (0, 0))) for q in range(GROUP)
    ]
    return jnp.stack(rows).reshape(GROUP * kernel.shape[2], -1)


def residual_block(rows, cols, features, first, second, scales):
    chans, height, width = features.shape
    count = height // STEP
    depth = count * chans
    x = jnp.transpose(features.reshape(chans, count, STEP, width), (2, 1, 0, 3))
    x = x.reshape(STEP, depth, width)
    full = depth + 2 * chans
    scales = jnp.broadcast_to(jnp.stack(scales)[:, :, None], (4, chans, LANES))
    vmem = pl.BlockSpec(memory_space=pltpu.VMEM)
    dma = pltpu.SemaphoreType.DMA
    summed = pl.pallas_call(
        functools.partial(block_kernel, rows, cols),
        out_shape=jax.ShapeDtypeStruct(x.shape, jnp.bfloat16),
        in_specs=[vmem] * 4,
        out_specs=vmem,
        scratch_shapes=[
            pltpu.VMEM((STEP, full, width + 2 * LANES), jnp.bfloat16),
            pltpu.VMEM((STEP, full, width + 2 * LANES), jnp.bfloat16),
            pltpu.VMEM((STEP, depth, width), jnp.float32),
            pltpu.VMEM((2, full, LANES), jnp.bfloat16),
            pltpu.VMEM((4, full, LANES), jnp.bfloat16),
            pltpu.VMEM((2 * cols, 2 * chans, LANES), jnp.float32),
            pltpu.VMEM((2 * rows, 2 * chans, LANES), jnp.float32),
            dma((4,)),
            dma((4,)),
            dma((4,)),
            dma((4,)),
            dma((2 * cols,)),
            dma((2 * cols,)),
            dma((2 * rows,)),
            dma((2 * rows,)),
        ],
        compiler_params=pltpu.CompilerParams(
            collective_id=0, has_side_effects=True, vmem_limit_bytes=48 * 1024 * 1024
        ),
    )(x, banded(first), banded(second), scales)
    summed = summed.reshape(STEP, count, chans, width)
    return jnp.transpose(summed, (2, 1, 0, 3)).reshape(features.shape)


def mirror(block):
    row_devs = lax.axis_size("row")
    col_devs = lax.axis_size("col")
    channels, tile_rows, tile_cols = block.shape
    ratio = row_devs // col_devs
    row = lax.axis_index("row")
    arranged = jnp.zeros((channels, tile_rows, tile_cols), block.dtype)
    for step in range(ratio):
        half = (step + row) % ratio
        part = lax.dynamic_slice_in_dim(block, half * tile_rows, tile_rows, axis=2)
        pairs = [
            (r * col_devs + c, (ratio * c + (step + r) % ratio) * col_devs + r // ratio)
            for r in range(row_devs)
            for c in range(col_devs)
        ]
        moved = jnp.swapaxes(lax.ppermute(part, ("row", "col"), pairs), 1, 2)
        place = (row - step) % ratio
        arranged = lax.dynamic_update_slice_in_dim(arranged, moved, place * tile_rows, axis=2)
    return arranged


def solution(mesh):
    rows, cols = mesh.shape["row"], mesh.shape["col"]

    def per_device(features, first, second, gain_one, shift_one, gain_two, shift_two):
        scales = (gain_one, shift_one, gain_two, shift_two)
        summed = residual_block(rows, cols, features, first, second, scales)
        total = summed.astype(jnp.float32) + mirror(summed).astype(jnp.float32)
        return (total * 0.5).astype(jnp.bfloat16)

    placed = (P(None, "row", "col"), P(), P(), P(), P(), P(), P())
    return jax.shard_map(
        per_device, mesh=mesh, in_specs=placed, out_specs=P(None, "row", "col"), check_vma=False
    )
```

profile of v0, /device:TPU:3, one launch (start us, length us, event | category | flops | bytes accessed | tf_op | source)
XLA Modules:
  0.0 219.3 jit_solution(4974297429960672701)
XLA Ops:
  0.0 1.1 pad_bitcast_fusion.7
  1.1 0.2 pad_maximum_fusion
  1.3 0.3 copy.21
  1.6 0.4 reshape.25.first_ref
  2.0 0.0 copy-done.1
  2.0 0.1 pad_bitcast_fusion.3
  2.1 0.2 pad_maximum_fusion.1
  2.3 0.3 copy.22
  2.5 0.4 reshape.26.second_ref
  3.0 0.0 copy-start.2
  3.0 0.0 copy-start.3
  3.0 0.0 copy-start.4
  3.0 0.0 copy-start.5
  3.0 2.8 %copy.13 = bf16[32,16,8,256]{3,0,1,2:T(8,128)(2,1)S(1)} copy(bf16[32,16,8,256]{3,2,1,0:T(8,128)(2,1)} %bitcast.40) | data formatting | bytes 4194304 | tf_op jit(solution)/shard_map/reshape | solution.py:290
  5.8 0.0 copy-done.2
  5.8 0.0 copy-done.3
  5.8 0.0 copy-done.4
  5.9 0.1 broadcast_in_dim.4.scales_ref
  5.9 62.8 %shard_map.73 = bf16[8,512,256]{2,1,0:T(8,128)(2,1)S(1)} custom-call(bf16[8,512,256]{2,1,0:T(8,128)(2,1)S(1)} %bitcast.38, bf16[128,576]{1,0:T(8,128)(2,1)S(1)} %reshape.25.first_ref, bf16[128,576]{1,0:T(8,128)(2,1)S(1)} %reshape.26.second_ref, f32[4,32,128]{2,1,0:T(8,128)S(1)} %broadcast_in_dim.4.scales_ref), custom_call_target="tpu_custom_call" | custom-call | tf_op jit(solution)/shard_map/pallas_call | solution.py:296
  68.8 2.5 %copy.28 = bf16[8,16,32,256]{3,0,1,2:T(8,128)(2,1)} copy(bf16[8,16,32,256]{3,2,1,0:T(8,128)(2,1)S(1)} %bitcast.36) | data formatting | bytes 4194304 | tf_op jit(solution)/shard_map/reshape | solution.py:322
  71.3 2.7 %constant_dynamic-slice_fusion = (bf16[32,128,128]{2,1,0:T(8,128)(2,1)S(1)}, bf16[32,128,128]{2,1,0:T(8,128)(2,1)}) fusion(bf16[32,128,256]{2,1,0:T(8,128)(2,1)} %bitcast.39, s32[]{:T(128)S(6)} %select_n.30, s32[]{:T(128)S(6)} %select_n.28), kind=kLoop, calls=%fused_computation.14 | loop fusion | bytes 4194312 | tf_op jit(solution)/shard_map/dynamic_slice | solution.py:335
  74.0 1.9 collective-permute-start.1
  75.9 2.7 %collective-permute-start = (bf16[32,128,128]{2,1,0:T(8,128)(2,1)}, bf16[32,128,128]{2,1,0:T(8,128)(2,1)}, u32[]{:S(2)}, u32[]{:S(2)}) collective-permute-start(bf16[32,128,128]{2,1,0:T(8,128)(2,1)} %get-tuple-element.6), channel_id=1, source_target_pairs={{0,0},{1,8},{2,16},{3,24},{4,4},{5,12},{6,20},{7,28},{8,1},{9,9},{... | collective-permute-start | bytes 3145736 | tf_op jit(solution)/shard_map/ppermute | solution.py:341
  78.7 111.5 %collective-permute-done.1 = bf16[32,128,128]{2,1,0:T(8,128)(2,1)} collective-permute-done((bf16[32,128,128]{2,1,0:T(8,128)(2,1)S(1)}, bf16[32,128,128]{2,1,0:T(8,128)(2,1)}, u32[]{:S(2)}, u32[]{:S(2)}) %collective-permute-start.1) | collective-permute-done | bytes 1048608 | tf_op jit(solution)/shard_map/ppermute | solution.py:341
  190.2 1.6 copy.20
  191.8 20.6 %collective-permute-done = bf16[32,128,128]{2,1,0:T(8,128)(2,1)} collective-permute-done((bf16[32,128,128]{2,1,0:T(8,128)(2,1)}, bf16[32,128,128]{2,1,0:T(8,128)(2,1)}, u32[]{:S(2)}, u32[]{:S(2)}) %collective-permute-start) | collective-permute-done | bytes 1048608 | tf_op jit(solution)/shard_map/ppermute | solution.py:341
  212.5 2.3 %copy.19 = bf16[32,128,128]{2,1,0:T(8,128)(2,1)} copy(bf16[32,128,128]{1,2,0:T(8,128)(2,1)} %bitcast.21) | data formatting | bytes 2097152 | tf_op jit(solution)/shard_map/transpose | solution.py:341
  214.7 0.2 broadcast_in_dim.10
  215.0 1.0 copy-done
  216.0 0.2 constant_dynamic-update-slice_fusion.1
  216.2 0.3 constant_dynamic-update-slice_fusion
  216.5 2.8 %multiply_convert_fusion = bf16[32,128,256]{2,1,0:T(8,128)(2,1)} fusion(bf16[32,128,256]{2,1,0:T(8,128)(2,1)S(1)} %constant_dynamic-update-slice_fusion, bf16[8,16,32,256]{3,2,1,0:T(8,128)(2,1)S(1)} %bitcast.37), kind=kLoop, calls=%fused_computation | loop fusion | flops 5242880 | bytes 6291456 | tf_op jit(solution)/shard_map/convert_element_type | solution.py:354
  (4 shorter events, 0.0 us)
Async XLA Ops:
  0.0 2.0 copy-start.1
  3.0 2.8 %copy-start.2 = (f32[32]{0:T(128)S(1)}, f32[32]{0:T(128)}, u32[]{:S(2)}) copy-start(f32[32]{0:T(128)} %param.13) | copy-start | bytes 388
  3.0 2.8 %copy-start.3 = (f32[32]{0:T(128)S(1)}, f32[32]{0:T(128)}, u32[]{:S(2)}) copy-start(f32[32]{0:T(128)} %param.12) | copy-start | bytes 388
  3.0 2.8 %copy-start.4 = (f32[32]{0:T(128)S(1)}, f32[32]{0:T(128)}, u32[]{:S(2)}) copy-start(f32[32]{0:T(128)} %param.11) | copy-start | bytes 388
  3.0 2.8 %copy-start.5 = (f32[32]{0:T(128)S(1)}, f32[32]{0:T(128)}, u32[]{:S(2)}) copy-start(f32[32]{0:T(128)} %param.10) | copy-start | bytes 388
  74.0 116.3 %collective-permute-start.1 = (bf16[32,128,128]{2,1,0:T(8,128)(2,1)S(1)}, bf16[32,128,128]{2,1,0:T(8,128)(2,1)}, u32[]{:S(2)}, u32[]{:S(2)}) collective-permute-start(bf16[32,128,128]{2,1,0:T(8,128)(2,1)S(1)} %get-tuple-element.5), channel_id=1, source_target_pairs={{0,4},{1,12},{2,20},{3,28},{4,0},{5,8},{6,16},{7,24},{8,5},{9,13},... | collective-permute-start | bytes 3145736 | tf_op jit(solution)/shard_map/ppermute | solution.py:341
  75.9 136.6 %collective-permute-start = (bf16[32,128,128]{2,1,0:T(8,128)(2,1)}, bf16[32,128,128]{2,1,0:T(8,128)(2,1)}, u32[]{:S(2)}, u32[]{:S(2)}) collective-permute-start(bf16[32,128,128]{2,1,0:T(8,128)(2,1)} %get-tuple-element.6), channel_id=1, source_target_pairs={{0,0},{1,8},{2,16},{3,24},{4,4},{5,12},{6,20},{7,28},{8,1},{9,9},{... | collective-permute-start | bytes 3145736 | tf_op jit(solution)/shard_map/ppermute | solution.py:341
  214.7 1.2 copy-start
where the time goes:
time: 220 us; the launch traced here: 219 us
  waiting for transfers between devices  132 us (60%)
  Pallas kernels  62.8 us (29%)
  local copies, waits for them, and re-layouts  16.3 us (7%)
  starting transfers between devices  4.67 us (2%)
  other arithmetic  3.13 us (1%)
    ppermute x2, waiting for transfers between devices, mirror(): moved = jnp.swapaxes(lax.ppermute(part, ('row', 'col'), pairs), 1, 2)  132 us
    pallas_call x1, Pallas kernels, residual_block(): pl.pallas_call(functools.partial(block_kernel, rows, cols), out_shape=jax...  62.8 us
    ppermute x2, starting transfers between devices, mirror(): moved = jnp.swapaxes(lax.ppermute(part, ('row', 'col'), pairs), 1, 2)  4.67 us
  transfers between devices with their start and end apart: 2, of which 2 were waited for; matrix products, arithmetic and copies ran while one was open for 1% of the time, Pallas kernels for 0%

commit v1 on v0

--- a/solution.py
+++ b/solution.py
@@ -323,25 +323,199 @@
     return jnp.transpose(summed, (2, 1, 0, 3)).reshape(features.shape)
 
 
-def mirror(block):
-    row_devs = lax.axis_size("row")
-    col_devs = lax.axis_size("col")
-    channels, tile_rows, tile_cols = block.shape
-    ratio = row_devs // col_devs
+def mirror_kernel(
+    rows, cols, chunks, s_ref, out_ref, got, relay, send, recv, relay_send, relay_recv
+):
     row = lax.axis_index("row")
-    arranged = jnp.zeros((channels, tile_rows, tile_cols), block.dtype)
-    for step in range(ratio):
-        half = (step + row) % ratio
-        part = lax.dynamic_slice_in_dim(block, half * tile_rows, tile_rows, axis=2)
-        pairs = [
-            (r * col_devs + c, (ratio * c + (step + r) % ratio) * col_devs + r // ratio)
-            for r in range(row_devs)
-            for c in range(col_devs)
-        ]
-        moved = jnp.swapaxes(lax.ppermute(part, ("row", "col"), pairs), 1, 2)
-        place = (row - step) % ratio
-        arranged = lax.dynamic_update_slice_in_dim(arranged, moved, place * tile_rows, axis=2)
-    return arranged
+    col = lax.axis_index("col")
+    ratio = rows // cols
+    chans, height, _ = s_ref.shape
+    pieces = len(chunks)
+    block = lax.div(row, ratio)
+    part = lax.rem(row, ratio)
+    relays = block == col
+
+    barrier = pltpu.get_barrier_semaphore()
+    for d in range(1, cols):
+        pl.semaphore_signal(
+            barrier, inc=1, device_id=(row, lax.rem(col + d, cols)), device_id_type=MESH
+        )
+    for d in range(1, rows):
+        pl.semaphore_signal(
+            barrier, inc=1, device_id=(lax.rem(row + d, rows), col), device_id_type=MESH
+        )
+    for h in range(ratio):
+
+        @pl.when(jnp.logical_not(relays))
+        def _(h=h):
+            pl.semaphore_signal(
+                barrier, inc=1, device_id=(ratio * col + h, block), device_id_type=MESH
+            )
+
+    pl.semaphore_wait(barrier, rows + cols - 2 + jnp.where(relays, 0, ratio))
+
+    def span(k):
+        low, size, _ = chunks[k]
+        return pl.ds(low, size)
+
+    def source(h, k):
+        return s_ref.at[span(k), :, pl.ds(h * height, height)]
+
+    def straight(h, k):
+        return pltpu.make_async_remote_copy(
+            src_ref=source(h, k),
+            dst_ref=got.at[part, span(k)],
+            send_sem=send.at[h * pieces + k],
+            recv_sem=recv.at[part * pieces + k],
+            device_id=(ratio * col + h, block),
+            device_id_type=MESH,
+        )
+
+    def arrive(j, k):
+        return pltpu.make_async_remote_copy(
+            src_ref=got.at[j, span(k)],
+            dst_ref=got.at[j, span(k)],
+            send_sem=send.at[j * pieces + k],
+            recv_sem=recv.at[j * pieces + k],
+            device_id=(row, col),
+            device_id_type=MESH,
+        )
+
+    def first_leg(h, k, via):
+        if via == "col":
+            slot = (lax.rem(col - block + cols, cols) - 1) * ratio + h
+            device = (row, block)
+        else:
+            slot = (lax.rem(block - col + cols, cols) - 1) * ratio + part
+            device = (ratio * col + h, col)
+        return pltpu.make_async_remote_copy(
+            src_ref=source(h, k),
+            dst_ref=relay.at[slot, span(k)],
+            send_sem=send.at[h * pieces + k],
+            recv_sem=relay_recv.at[slot * pieces + k],
+            device_id=device,
+            device_id_type=MESH,
+        )
+
+    def second_leg(d, e, k, via):
+        slot = (d - 1) * ratio + e
+        other = lax.rem(col + d, cols)
+        if via == "col":
+            device = (ratio * other + e, col)
+            target = part
+        else:
+            device = (row, other)
+            target = e
+        return pltpu.make_async_remote_copy(
+            src_ref=relay.at[slot, span(k)],
+            dst_ref=got.at[target, span(k)],
+            send_sem=relay_send.at[slot * pieces + k],
+            recv_sem=recv.at[target * pieces + k],
+            device_id=device,
+            device_id_type=MESH,
+        )
+
+    @pl.when(jnp.logical_not(relays))
+    def _():
+        for k in range(pieces):
+            for h in range(ratio):
+                via = chunks[k][2]
+                (first_leg(h, k, via) if via else straight(h, k)).start()
+
+    @pl.when(relays)
+    def _():
+        for h in range(ratio):
+
+            @pl.when(part != h)
+            def _(h=h):
+                for k in range(pieces):
+                    straight(h, k).start()
+
+            @pl.when(part == h)
+            def _(h=h):
+                got[h] = s_ref[:, :, h * height : (h + 1) * height]
+
+        for k in range(pieces):
+            via = chunks[k][2]
+            if via:
+                for d in range(1, cols):
+                    for e in range(ratio):
+                        leg = second_leg(d, e, k, via)
+                        slot = (d - 1) * ratio + e
+                        pltpu.make_async_remote_copy(
+                            src_ref=relay.at[slot, span(k)],
+                            dst_ref=relay.at[slot, span(k)],
+                            send_sem=relay_send.at[slot * pieces + k],
+                            recv_sem=relay_recv.at[slot * pieces + k],
+                            device_id=(row, col),
+                            device_id_type=MESH,
+                        ).wait_recv()
+                        leg.start()
+
+    order = [k for k in range(pieces) if not chunks[k][2]]
+    order += [k for k in range(pieces) if chunks[k][2]]
+    for k in order:
+        for j in range(ratio):
+
+            @pl.when(jnp.logical_not(relays & (part == j)))
+            def _(j=j, k=k):
+                arrive(j, k).wait_recv()
+
+            low, size, _ = chunks[k]
+            at = pl.ds(j * height, height)
+
+            def body(c, carry, j=j, at=at):
+                turned = jnp.swapaxes(got[j, c].astype(jnp.float32), 0, 1)
+                total = s_ref[c, :, at].astype(jnp.float32) + turned
+                out_ref[c, :, at] = (total * 0.5).astype(jnp.bfloat16)
+                return carry
+
+            lax.fori_loop(low, low + size, body, 0)
+
+    for k in range(pieces):
+        for h in range(ratio):
+
+            @pl.when(jnp.logical_not(relays & (part == h)))
+            def _(h=h, k=k):
+                straight(h, k).wait_send()
+
+    @pl.when(relays)
+    def _():
+        for k in range(pieces):
+            via = chunks[k][2]
+            if via:
+                for d in range(1, cols):
+                    for e in range(ratio):
+                        second_leg(d, e, k, via).wait_send()
+
+
+CHUNKS = ((16, 4, "row"), (20, 4, "row"), (24, 4, "row"), (28, 4, "row"), (0, 8, ""), (8, 8, ""))
+
+
+def symmetrize(rows, cols, summed):
+    chans, height, width = summed.shape
+    ratio = rows // cols
+    pieces = len(CHUNKS)
+    slots = (cols - 1) * ratio
+    vmem = pl.BlockSpec(memory_space=pltpu.VMEM)
+    dma = pltpu.SemaphoreType.DMA
+    return pl.pallas_call(
+        functools.partial(mirror_kernel, rows, cols, CHUNKS),
+        out_shape=jax.ShapeDtypeStruct(summed.shape, jnp.bfloat16),
+        in_specs=[vmem],
+        out_specs=vmem,
+        scratch_shapes=[
+            pltpu.VMEM((ratio, chans, height, height), jnp.bfloat16),
+            pltpu.VMEM((slots, chans, height, height), jnp.bfloat16),
+            dma((ratio * pieces,)),
+            dma((ratio * pieces,)),
+            dma((slots * pieces,)),
+            dma((slots * pieces,)),
+        ],
+        compiler_params=pltpu.CompilerParams(
+            collective_id=1, has_side_effects=True, vmem_limit_bytes=48 * 1024 * 1024
+        ),
+    )(summed)
 
 
 def solution(mesh):
@@ -350,8 +524,7 @@
     def per_device(features, first, second, gain_one, shift_one, gain_two, shift_two):
         scales = (gain_one, shift_one, gain_two, shift_two)
         summed = residual_block(rows, cols, features, first, second, scales)
-        total = summed.astype(jnp.float32) + mirror(summed).astype(jnp.float32)
-        return (total * 0.5).astype(jnp.bfloat16)
+        return symmetrize(rows, cols, summed)
 
     placed = (P(None, "row", "col"), P(), P(), P(), P(), P(), P())
     return jax.shard_map(

time: 220 us -> 166 us (0.75)
  the two profiles are of different devices: /device:TPU:3 before, /device:TPU:0 now
where the time goes in v1:
time: 166 us; the launch traced here: 164 us
  Pallas kernels  156 us (94%)
  local copies, waits for them, and re-layouts  6.95 us (4%)
    pallas_call x1, Pallas kernels, symmetrize(): pl.pallas_call(functools.partial(mirror_kernel, rows, cols, CHUNKS), out_...  91.2 us
    pallas_call x1, Pallas kernels, residual_block(): pl.pallas_call(functools.partial(block_kernel, rows, cols), out_shape=jax...  64.7 us

profile of v1, /device:TPU:0, one launch (start us, length us, event | category | flops | bytes accessed | tf_op | source)
XLA Modules:
  0.0 164.0 jit_solution(11946448011853816616)
XLA Ops:
  0.0 0.7 pad_maximum_fusion.2
  0.7 0.1 broadcast_in_dim.2.scales_ref
  0.8 0.0 copy-start.1
  0.8 1.1 pad_bitcast_fusion.7
  1.9 0.2 pad_maximum_fusion
  2.1 0.3 copy.18
  2.4 0.4 reshape.25.first_ref
  2.8 0.0 copy-done.1
  2.8 0.0 copy-start
  2.8 0.1 pad_bitcast_fusion.3
  2.9 0.2 pad_maximum_fusion.1
  3.1 0.3 copy.19
  3.3 0.4 reshape.26.second_ref
  3.8 0.6 copy-done
  4.4 1.2 copy.12
  5.6 64.7 %shard_map.73 = bf16[8,512,256]{2,1,0:T(8,128)(2,1)S(1)} custom-call(bf16[8,512,256]{2,1,0:T(8,128)(2,1)S(1)} %bitcast.33, bf16[128,576]{1,0:T(8,128)(2,1)S(1)} %reshape.25.first_ref, bf16[128,576]{1,0:T(8,128)(2,1)S(1)} %reshape.26.second_ref, f32[4,32,128]{2,1,0:T(8,128)S(1)} %broadcast_in_dim.2.scales_ref), custom_call_target="tpu_custom_call" | custom-call | tf_op jit(solution)/shard_map/pallas_call | solution.py:296
  70.3 1.2 copy.23
  71.5 91.2 %shard_map.74 = bf16[32,128,256]{2,1,0:T(8,128)(2,1)S(1)} custom-call(bf16[32,128,256]{2,1,0:T(8,128)(2,1)S(1)} %bitcast.34), custom_call_target="tpu_custom_call" | custom-call | tf_op jit(solution)/shard_map/pallas_call | solution.py:502
  162.7 1.3 copy.25
Async XLA Ops:
  0.8 2.0 %copy-start.1 = (bf16[3,3,32,32]{3,2,1,0:T(8,128)(2,1)S(1)}, bf16[3,3,32,32]{3,2,1,0:T(8,128)(2,1)}, u32[]{:S(2)}) copy-start(bf16[3,3,32,32]{3,2,1,0:T(8,128)(2,1)} %param.9) | copy-start | bytes 55300
  2.8 1.6 copy-start

commit v2 on v1

--- a/solution.py
+++ b/solution.py
@@ -354,8 +354,17 @@
 
     pl.semaphore_wait(barrier, rows + cols - 2 + jnp.where(relays, 0, ratio))
 
+    def direct(source_col, source_block):
+        z, p = lax.rem(source_col, 4), lax.rem(source_block, 4)
+        chosen = (z == p) & (lax.rem(source_col + source_block, 8) < 4)
+        for a, b in DIRECT:
+            chosen = chosen | ((z == a) & (p == b))
+        return chosen
+
+    mine = direct(col, block)
+
     def span(k):
-        low, size, _ = chunks[k]
+        low, size = chunks[k]
         return pl.ds(low, size)
 
     def source(h, k):
@@ -381,46 +390,39 @@
             device_id_type=MESH,
         )
 
-    def first_leg(h, k, via):
-        if via == "col":
-            slot = (lax.rem(col - block + cols, cols) - 1) * ratio + h
-            device = (row, block)
-        else:
-            slot = (lax.rem(block - col + cols, cols) - 1) * ratio + part
-            device = (ratio * col + h, col)
+    def first_leg(h, k):
+        slot = (lax.rem(block - col + cols, cols) - 1) * ratio + part
         return pltpu.make_async_remote_copy(
             src_ref=source(h, k),
             dst_ref=relay.at[slot, span(k)],
             send_sem=send.at[h * pieces + k],
             recv_sem=relay_recv.at[slot * pieces + k],
-            device_id=device,
+            device_id=(ratio * col + h, col),
             device_id_type=MESH,
         )
 
-    def second_leg(d, e, k, via):
+    def second_leg(d, e, k):
         slot = (d - 1) * ratio + e
-        other = lax.rem(col + d, cols)
-        if via == "col":
-            device = (ratio * other + e, col)
-            target = part
-        else:
-            device = (row, other)
-            target = e
         return pltpu.make_async_remote_copy(
             src_ref=relay.at[slot, span(k)],
-            dst_ref=got.at[target, span(k)],
+            dst_ref=got.at[e, span(k)],
             send_sem=relay_send.at[slot * pieces + k],
-            recv_sem=recv.at[target * pieces + k],
-            device_id=device,
+            recv_sem=recv.at[e * pieces + k],
+            device_id=(row, lax.rem(col + d, cols)),
             device_id_type=MESH,
         )
 
-    @pl.when(jnp.logical_not(relays))
+    @pl.when(jnp.logical_not(relays) & mine)
     def _():
         for k in range(pieces):
             for h in range(ratio):
-                via = chunks[k][2]
-                (first_leg(h, k, via) if via else straight(h, k)).start()
+                straight(h, k).start()
+
+    @pl.when(jnp.logical_not(relays | mine))
+    def _():
+        for k in range(pieces):
+            for h in range(ratio):
+                first_leg(h, k).start()
 
     @pl.when(relays)
     def _():
@@ -436,11 +438,11 @@
                 got[h] = s_ref[:, :, h * height : (h + 1) * height]
 
         for k in range(pieces):
-            via = chunks[k][2]
-            if via:
-                for d in range(1, cols):
+            for d in range(1, cols):
+
+                @pl.when(jnp.logical_not(direct(col, lax.rem(col + d, cols))))
+                def _(d=d, k=k):
                     for e in range(ratio):
-                        leg = second_leg(d, e, k, via)
                         slot = (d - 1) * ratio + e
                         pltpu.make_async_remote_copy(
                             src_ref=relay.at[slot, span(k)],
@@ -450,18 +452,16 @@
                             device_id=(row, col),
                             device_id_type=MESH,
                         ).wait_recv()
-                        leg.start()
-
-    order = [k for k in range(pieces) if not chunks[k][2]]
-    order += [k for k in range(pieces) if chunks[k][2]]
-    for k in order:
+                        second_leg(d, e, k).start()
+
+    for k in range(pieces):
         for j in range(ratio):
 
             @pl.when(jnp.logical_not(relays & (part == j)))
             def _(j=j, k=k):
                 arrive(j, k).wait_recv()
 
-            low, size, _ = chunks[k]
+            low, size = chunks[k]
             at = pl.ds(j * height, height)
 
             def body(c, carry, j=j, at=at):
@@ -482,25 +482,28 @@
     @pl.when(relays)
     def _():
         for k in range(pieces):
-            via = chunks[k][2]
-            if via:
-                for d in range(1, cols):
+            for d in range(1, cols):
+
+                @pl.when(jnp.logical_not(direct(col, lax.rem(col + d, cols))))
+                def _(d=d, k=k):
                     for e in range(ratio):
-                        second_leg(d, e, k, via).wait_send()
-
-
-CHUNKS = ((16, 4, "row"), (20, 4, "row"), (24, 4, "row"), (28, 4, "row"), (0, 8, ""), (8, 8, ""))
+                        second_leg(d, e, k).wait_send()
+
+
+DIRECT = ((0, 1), (0, 2), (1, 3), (2, 0), (3, 1), (3, 2))
 
 
 def symmetrize(rows, cols, summed):
     chans, height, width = summed.shape
     ratio = rows // cols
-    pieces = len(CHUNKS)
+    size = 4 if chans % 4 == 0 else chans
+    chunks = tuple((low, size) for low in range(0, chans, size))
+    pieces = len(chunks)
     slots = (cols - 1) * ratio
     vmem = pl.BlockSpec(memory_space=pltpu.VMEM)
     dma = pltpu.SemaphoreType.DMA
     return pl.pallas_call(
-        functools.partial(mirror_kernel, rows, cols, CHUNKS),
+        functools.partial(mirror_kernel, rows, cols, chunks),
         out_shape=jax.ShapeDtypeStruct(summed.shape, jnp.bfloat16),
         in_specs=[vmem],
         out_specs=vmem,

time: 166 us -> 131 us (0.79)
  Pallas kernels: 156 us -> 121 us
    pallas_call x1, Pallas kernels: 91.2 us -> 56.4 us  [symmetrize(): pl.pallas_call(functools.partial(mirror_kernel, rows, cols, chunks), out_...]
where the time goes in v2:
time: 131 us; the launch traced here: 129 us
  Pallas kernels  121 us (92%)
  local copies, waits for them, and re-layouts  6.95 us (5%)
    pallas_call x1, Pallas kernels, residual_block(): pl.pallas_call(functools.partial(block_kernel, rows, cols), out_shape=jax...  64.7 us
    pallas_call x1, Pallas kernels, symmetrize(): pl.pallas_call(functools.partial(mirror_kernel, rows, cols, chunks), out_...  56.4 us

profile of v2, /device:TPU:0, one launch (start us, length us, event | category | flops | bytes accessed | tf_op | source)
XLA Modules:
  0.0 129.2 jit_solution(7322063152138313404)
XLA Ops:
  0.0 0.7 pad_maximum_fusion.2
  0.7 0.1 broadcast_in_dim.2.scales_ref
  0.8 0.0 copy-start.1
  0.8 1.1 pad_bitcast_fusion.7
  1.9 0.2 pad_maximum_fusion
  2.1 0.3 copy.18
  2.4 0.4 reshape.25.first_ref
  2.8 0.0 copy-done.1
  2.8 0.0 copy-start
  2.8 0.1 pad_bitcast_fusion.3
  2.9 0.2 pad_maximum_fusion.1
  3.1 0.3 copy.19
  3.3 0.4 reshape.26.second_ref
  3.8 0.6 copy-done
  4.4 1.2 copy.12
  5.6 64.7 %shard_map.73 = bf16[8,512,256]{2,1,0:T(8,128)(2,1)S(1)} custom-call(bf16[8,512,256]{2,1,0:T(8,128)(2,1)S(1)} %bitcast.33, bf16[128,576]{1,0:T(8,128)(2,1)S(1)} %reshape.25.first_ref, bf16[128,576]{1,0:T(8,128)(2,1)S(1)} %reshape.26.second_ref, f32[4,32,128]{2,1,0:T(8,128)S(1)} %broadcast_in_dim.2.scales_ref), custom_call_target="tpu_custom_call" | custom-call | tf_op jit(solution)/shard_map/pallas_call | solution.py:296
  70.3 1.2 copy.23
  71.5 56.4 %shard_map.74 = bf16[32,128,256]{2,1,0:T(8,128)(2,1)S(1)} custom-call(bf16[32,128,256]{2,1,0:T(8,128)(2,1)S(1)} %bitcast.34), custom_call_target="tpu_custom_call" | custom-call | tf_op jit(solution)/shard_map/pallas_call | solution.py:505
  127.9 1.3 %copy.25 = bf16[32,128,256]{2,1,0:T(8,128)(2,1)} copy(bf16[32,128,256]{2,1,0:T(8,128)(2,1)S(1)} %shard_map.74) | data formatting | bytes 4194304
Async XLA Ops:
  0.8 2.0 %copy-start.1 = (bf16[3,3,32,32]{3,2,1,0:T(8,128)(2,1)S(1)}, bf16[3,3,32,32]{3,2,1,0:T(8,128)(2,1)}, u32[]{:S(2)}) copy-start(bf16[3,3,32,32]{3,2,1,0:T(8,128)(2,1)} %param.9) | copy-start | bytes 55300
  2.8 1.6 %copy-start = (bf16[32,128,256]{2,1,0:T(8,128)(2,1)S(1)}, bf16[32,128,256]{2,1,0:T(8,128)(2,1)}, u32[]{:S(2)}) copy-start(bf16[32,128,256]{2,1,0:T(8,128)(2,1)} %param.7) | copy-start | bytes 6291460
